TPU v7x, 32 devices: a whole 2x2x4 slice. The times are simulated.
32 devices in a mesh: pair: 4 (over y, core), virt: 8 (over z, x).
Axes of the slice: x: 2, y: 2, z: 4, core: 2. Of those that a mesh axis runs over, the one named last changes fastest.
Arguments:
- amplitudes: float32 [4096, 1024], P('pair', 'virt'), may hold values from -6 to 6
- integrals: float32 [8192, 1024], P('virt', 'pair'), may hold values from -0.54 to 0.54
- residual_in: float32 [4096, 8192], P('pair', 'virt'), may hold values from -6 to 6
- pair_irrep: int32 [4096], P('pair'), may hold values from 0 to 7
- ab_irrep: int32 [8192], P('virt'), may hold values from 0 to 7
- cd_irrep: int32 [1024], replicated, may hold values from 0 to 7, as said below
Outputs:
- residual: float32 [4096, 8192], P('pair', 'virt')
Inputs may be any that keep to these rules, and one draw needn't show every extreme that they name: `pair_irrep`: irrep labels. `ab_irrep`: irrep labels. `cd_irrep`: in every aligned block of 8 consecutive cd of the window, each of the 8 irreps labels exactly one cd.
All inputs are finite; a program needn't handle non-finite values.
Results may differ from a plain program's by a relative error of at most 0.00005.
Values sent between devices are 32-bit elements; how exact they have to be, the bound alone decides.
A program may use at most 64 MiB of HBM per device.

v0:
```python
import jax
import jax.numpy as jnp
from jax import lax
from jax.sharding import PartitionSpec as P


def contract(left, right):
    return lax.dot_general(
        left,
        right,
        (((1,), (1,)), ((), ())),
        precision=lax.Precision.HIGHEST,
        preferred_element_type=jnp.float32,
    )


def shards(amplitudes, integrals, residual_in, pair_irrep, ab_irrep, cd_irrep):
    full_t = lax.all_gather(amplitudes, "virt", axis=1, tiled=True)
    masked_t = jnp.where(pair_irrep[:, None] == cd_irrep[None, :], full_t, jnp.float32(0.0))
    masked_v = jnp.where(
        ab_irrep[:, None] == cd_irrep[None, :],
        lax.all_gather(integrals, "pair", axis=1, tiled=True),
        jnp.float32(0.0),
    )
    return residual_in + contract(masked_t, masked_v)


def solution(mesh):
    placed = (P("pair", "virt"), P("virt", "pair"), P("pair", "virt"), P("pair"), P("virt"), P())
    return jax.shard_map(
        shards, mesh=mesh, in_specs=placed, out_specs=P("pair", "virt"), check_vma=False
    )
```

profile of v0, /device:TPU:0, one launch (start us, length us, event | category | flops | bytes accessed | tf_op | source)
XLA Modules:
  0.0 149.9 jit_solution(6792868055530968474)
XLA Ops:
  6.5 0.0 all-gather.5.cloned.1.call-start
  6.5 0.7 all-gather.5.cloned.1.call-update
  7.3 0.0 all-gather.3.cloned.1.call-start
  7.3 0.7 all-gather.3.cloned.1.call-update
  8.0 38.1 %all-gather.5.cloned.1.call-done = f32[1024,1024]{1,0:T(8,128)} async-done(((f32[1024,256]{1,0:T(8,128)}), f32[1024,1024]{1,0:T(8,128)}) %all-gather.5.cloned.1.call-update) | async-done | bytes 4194320 | tf_op jit(solution)/shard_map/all_gather | solution.py:22
  46.1 77.1 %all-gather.3.cloned.1.call-done = f32[1024,1024]{1,0:T(8,128)} async-done(((f32[1024,128]{1,0:T(8,128)}), f32[1024,1024]{1,0:T(8,128)}) %all-gather.3.cloned.1.call-update) | async-done | bytes 4194320 | tf_op jit(solution)/shard_map/all_gather | solution.py:18
  123.2 19.8 %fusion.9 = f32[1024,1024]{1,0:T(8,128)} fusion(f32[1024,1024]{1,0:T(8,128)} %param.8, f32[1024,1024]{1,0:T(8,128)} %all-gather.5.cloned.1.call-done, s32[1024]{0:T(1024)} %param.11, s32[1024]{0:T(1024)} %param.10, f32[1024,1024]{1,0:T(8,128)} %all-gather.3.cloned.1.call-done, s32[1024]{0:T(1024)} %param.9), kind=kOutput, calls=%fused_computation.9 | convolution fusion | flops 12890144768 | bytes 16789504 | tf_op jit(solution)/shard_map/dot_general | solution.py:8
Async XLA Ops:
  6.5 39.6 %all-gather.5.cloned.1.call-start = ((), (), s32[]{:S(2)}) async-start(), calls=%async_computation.1 | async-start | bytes 5242880 | tf_op jit(solution)/shard_map/all_gather | solution.py:22
  7.3 116.0 %all-gather.3.cloned.1.call-start = ((), (), s32[]{:S(2)}) async-start(), calls=%async_computation | async-start | bytes 4718592 | tf_op jit(solution)/shard_map/all_gather | solution.py:18
Sparse Core Ops, SparseCore 0:
  8.9 37.1 all-gather.4
  48.2 75.0 all-gather.2
where the time goes:
time: 150 us
  waiting for transfers between devices  117 us (78%)
  matrix products  19.8 us (13%)
  between operations  13.4 us (9%)
    all_gather x1, waiting for transfers between devices, shards(): full_t = lax.all_gather(amplitudes, 'virt', axis=1, tiled=True)  77.1 us
    all_gather x1, waiting for transfers between devices, shards(): lax.all_gather(integrals, 'pair', axis=1, tiled=True)  38.1 us
    dot_general x1, matrix products, contract(): lax.dot_general(left, right, (((1,), (1,)), ((), ())), precision=lax.Prec...  19.8 us
  transfers between devices with their start and end apart: 2, of which 2 were waited for; matrix products, arithmetic and copies ran while one was open for 0% of the time, Pallas kernels for 0%

commit v1 on v0

v1 whole, which is shorter than its diff:
```python
import functools

import jax
import jax.numpy as jnp
from jax import lax
from jax.experimental import pallas as pl
from jax.experimental.pallas import tpu as pltpu
from jax.sharding import PartitionSpec as P

IRREPS = 8
LANES = 128
MESH = pl.DeviceIdType.MESH


def pieces(x):
    high = x.astype(jnp.bfloat16)
    low = (x - high.astype(jnp.float32)).astype(jnp.bfloat16)
    return high, low


def nth_other(n, me, step):
    flip = me // (n // 2)
    mine = me + flip * (n - 1 - 2 * me)
    other = step + (step + n - mine) // n
    return other + flip * (n - 1 - 2 * other)


def irrep_row(rows_ref, first, count):
    n = count // LANES
    return jnp.concatenate([rows_ref[pl.ds(first + k, 1), :] for k in range(n)], axis=1)


def pick(cd_row, values, own_row):
    width = values.shape[1]
    blocks = width // IRREPS
    block = lax.broadcasted_iota(jnp.int32, (blocks, width), 0)
    lane_block = lax.shift_right_logical(lax.broadcasted_iota(jnp.int32, (blocks, width), 1), 3)
    slabs = [
        jnp.where((block == lane_block) & (cd_row == g), jnp.float32(1), jnp.float32(0))
        for g in range(IRREPS)
    ]
    sorter = jnp.concatenate(slabs, axis=0).astype(jnp.bfloat16)
    high, low = pieces(values)
    across = (((1,), (1,)), ((), ()))
    by_irrep = lax.dot_general(
        sorter, high, across, preferred_element_type=jnp.float32
    ) + lax.dot_general(sorter, low, across, preferred_element_type=jnp.float32)
    chosen = by_irrep[:blocks]
    for g in range(1, IRREPS):
        chosen = jnp.where(own_row == g, by_irrep[g * blocks : (g + 1) * blocks], chosen)
    return chosen


def gather_kernel(
    n_pair, n_virt, parts,
    t_hbm, v_hbm, pi_ref, ai_ref, cdt_ref, cdv_ref,
    t_out, v_out,
    t_own, v_own, t_all, v_all,
    load_sem, t_send, t_recv, tf_send, v_send, v_recv, vf_send,
):
    p, v = lax.axis_index("pair"), lax.axis_index("virt")
    a, b = v // 2, v % 2
    c, k = p // 2, p % 2
    n_a, n_c = n_virt // 2, n_pair // 2
    rows, t_width = t_own.shape
    ab, v_width = v_own.shape
    t_blocks, v_blocks = t_width // IRREPS, v_width // IRREPS

    load_t = pltpu.make_async_copy(t_hbm, t_own, load_sem.at[0])
    load_v = pltpu.make_async_copy(v_hbm, v_own, load_sem.at[1])
    load_t.start()
    load_v.start()

    barrier = pltpu.get_barrier_semaphore()

    def greet(dev):
        pl.semaphore_signal(barrier, inc=1, device_id=dev, device_id_type=MESH)

    far_a = [nth_other(n_a, a, s) for s in range(n_a - 1)]
    far_c = [nth_other(n_c, c, s) for s in range(n_c - 1)]
    for o in far_a:
        greet((p, o * 2 + b))
    greet((p, a * 2 + 1 - b))
    for o in far_c:
        greet((o * 2 + k, v))
    greet((c * 2 + 1 - k, v))

    def copy(ref, owner, blocks, part, span, send, recv, dev):
        at = ref.at[pl.ds(pl.multiple_of(owner * blocks, blocks), blocks), pl.ds(part * span, span)]
        return pltpu.make_async_remote_copy(
            src_ref=at, dst_ref=at, send_sem=send, recv_sem=recv, device_id=dev, device_id_type=MESH
        )

    t_span, v_span = rows // parts, ab // parts

    def t_copy(owner, part, send, dev):
        return copy(t_all, owner, t_blocks, part, t_span, send, t_recv.at[owner * parts + part], dev)

    def v_copy(owner, part, send, dev):
        return copy(v_all, owner, v_blocks, part, v_span, send, v_recv.at[owner * parts + part], dev)

    cdt_row = irrep_row(cdt_ref, v * t_width // LANES, t_width) if t_width % LANES == 0 else cdt_ref[pl.ds(v, 1), :]
    cdv_row = irrep_row(cdv_ref, p * v_width // LANES, v_width) if v_width % LANES == 0 else cdv_ref[pl.ds(p, 1), :]

    load_t.wait()
    sent = []
    for h in range(parts):
        own = irrep_row(pi_ref, h * t_span // LANES, t_span)
        t_all[pl.ds(pl.multiple_of(v * t_blocks, t_blocks), t_blocks), h * t_span : (h + 1) * t_span] = pick(
            cdt_row, t_own[h * t_span : (h + 1) * t_span, :], own
        )
        if h == 0:
            pl.semaphore_wait(barrier, n_a + n_c)
        for s in reversed(range(n_a - 1)):
            sent.append(t_copy(v, h, t_send.at[s, h], (p, far_a[s] * 2 + b)))
            sent[-1].start()
        sent.append(t_copy(v, h, t_send.at[n_a - 1, h], (p, a * 2 + 1 - b)))
        sent[-1].start()

    load_v.wait()
    for h in range(parts):
        own = irrep_row(ai_ref, h * v_span // LANES, v_span)
        v_all[pl.ds(pl.multiple_of(p * v_blocks, v_blocks), v_blocks), h * v_span : (h + 1) * v_span] = pick(
            cdv_row, v_own[h * v_span : (h + 1) * v_span, :], own
        )
        for s in reversed(range(n_c - 1)):
            sent.append(v_copy(p, h, v_send.at[s, h], (far_c[s] * 2 + k, v)))
            sent[-1].start()
        sent.append(v_copy(p, h, v_send.at[n_c - 1, h], (c * 2 + 1 - k, v)))
        sent[-1].start()

    for h in range(parts):
        for s in range(n_a - 1):
            dev = (p, a * 2 + 1 - b)
            onward = t_copy(far_a[s] * 2 + b, h, tf_send.at[s, h], dev)
            onward.wait_recv()
            onward.start()
            sent.append(onward)
        for s in range(n_c - 1):
            dev = (c * 2 + 1 - k, v)
            onward = v_copy(far_c[s] * 2 + k, h, vf_send.at[s, h], dev)
            onward.wait_recv()
            onward.start()
            sent.append(onward)

    for h in range(parts):
        span = slice(h * v_span, (h + 1) * v_span)
        for o in range(n_c):
            v_copy(o * 2 + 1 - k, h, v_send.at[0, h], (p, v)).wait_recv()
        high, low = pieces(v_all[:, span])
        v_out[: high.shape[0], span] = high
        v_out[high.shape[0] :, span] = low
    for h in range(parts):
        span = slice(h * t_span, (h + 1) * t_span)
        for o in range(n_a):
            t_copy(o * 2 + 1 - b, h, t_send.at[0, h], (p, v)).wait_recv()
        t_out[:, span] = t_all[:, span]
    for s in sent:
        s.wait_send()


def gather(n_pair, n_virt, t, v, pi, ai, cd, cdt, cdv):
    parts = 2
    rows, t_width = t.shape
    ab, v_width = v.shape
    blocks = cd // IRREPS
    vmem, dma = pltpu.VMEM, pltpu.SemaphoreType.DMA
    n_a, n_c = n_virt // 2, n_pair // 2
    return pl.pallas_call(
        functools.partial(gather_kernel, n_pair, n_virt, parts),
        out_shape=(
            jax.ShapeDtypeStruct((blocks, rows), jnp.float32),
            jax.ShapeDtypeStruct((2 * blocks, ab), jnp.bfloat16),
        ),
        in_specs=[pl.BlockSpec(memory_space=pltpu.HBM)] * 2 + [pl.BlockSpec(memory_space=vmem)] * 4,
        out_specs=(pl.BlockSpec(memory_space=vmem),) * 2,
        scratch_shapes=[
            vmem((rows, t_width), jnp.float32),
            vmem((ab, v_width), jnp.float32),
            vmem((blocks, rows), jnp.float32),
            vmem((blocks, ab), jnp.float32),
            dma((2,)),
            dma((n_a, parts)),
            dma((n_virt * parts,)),
            dma((max(n_a - 1, 1), parts)),
            dma((n_c, parts)),
            dma((n_pair * parts,)),
            dma((max(n_c - 1, 1), parts)),
        ],
        compiler_params=pltpu.CompilerParams(
            collective_id=0, has_side_effects=True, vmem_limit_bytes=16 * 1024 * 1024
        ),
        name="pick_and_gather",
    )(t, v, pi, ai, cdt, cdv)


def ladder_kernel(t_ref, v_ref, pi_ref, ai_ref, r_ref, out_ref):
    blocks, tile = t_ref.shape
    ab = r_ref.shape[1]
    step = pl.program_id(0)
    th, tl = pieces(t_ref[...].T)
    left = jnp.concatenate([th, tl, th, tl], axis=1)
    vh, vl = v_ref[:blocks, :], v_ref[blocks:, :]
    right = jnp.concatenate([vh, vh, vl, vl], axis=0)
    total = lax.dot_general(left, right, (((1,), (0,)), ((), ())), preferred_element_type=jnp.float32)
    ab_row = irrep_row(ai_ref, 0, ab)
    for m in range(tile // LANES):
        row = pi_ref[pl.ds(step * (tile // LANES) + m, 1), :]
        column = jnp.broadcast_to(row, (LANES, LANES)).T
        same = jnp.concatenate([column] * (ab // LANES), axis=1) == ab_row
        at = slice(m * LANES, (m + 1) * LANES)
        out_ref[at, :] = r_ref[at, :] + jnp.where(same, total[at, :], jnp.float32(0))


def ladder(t_all, v_all, pi, ai, residual):
    rows, ab = residual.shape
    blocks = t_all.shape[0]
    tile = 256
    whole = lambda i: (0, 0)
    return pl.pallas_call(
        ladder_kernel,
        out_shape=jax.ShapeDtypeStruct((rows, ab), jnp.float32),
        grid=(rows // tile,),
        in_specs=[
            pl.BlockSpec((blocks, tile), lambda i: (0, i)),
            pl.BlockSpec(v_all.shape, whole),
            pl.BlockSpec(pi.shape, whole),
            pl.BlockSpec(ai.shape, whole),
            pl.BlockSpec((tile, ab), lambda i: (i, 0)),
        ],
        out_specs=pl.BlockSpec((tile, ab), lambda i: (i, 0)),
        compiler_params=pltpu.CompilerParams(vmem_limit_bytes=24 * 1024 * 1024),
        name="ladder",
    )(t_all, v_all, pi, ai, residual)


def solution(mesh):
    n_pair, n_virt = mesh.shape["pair"], mesh.shape["virt"]

    def shards(amplitudes, integrals, residual_in, pair_irrep, ab_irrep, cd_irrep):
        cd = cd_irrep.shape[0]
        pi, ai = pair_irrep.reshape(-1, LANES), ab_irrep.reshape(-1, LANES)

        def cd_rows(width):
            return cd_irrep.reshape(-1, LANES if width % LANES == 0 else width)

        t_all, v_all = gather(
            n_pair, n_virt, amplitudes, integrals, pi, ai, cd,
            cd_rows(amplitudes.shape[1]), cd_rows(integrals.shape[1]),
        )
        return ladder(t_all, v_all, pi, ai, residual_in)

    placed = (P("pair", "virt"), P("virt", "pair"), P("pair", "virt"), P("pair"), P("virt"), P())
    return jax.shard_map(
        shards, mesh=mesh, in_specs=placed, out_specs=P("pair", "virt"), check_vma=False
    )
```

time: 150 us -> 27.4 us (0.18)
  waiting for transfers between devices: 117 us -> 0 us
  matrix products: 19.8 us -> 0 us
  Pallas kernels: 0 us -> 19.1 us
  between operations: 13.4 us -> 0.02 us
  local copies, waits for them, and re-layouts: 0 us -> 7.88 us
    all_gather x2 -> x0, waiting for transfers between devices: 115 us -> none  [the longest x1 77.1 us: shards(): full_t = lax.all_gather(amplitudes, 'virt', axis=1, tiled=True)]
    dot_general x1 -> x0, matrix products: 19.8 us -> none  [contract(): lax.dot_general(left, right, (((1,), (1,)), ((), ())), precision=lax.Prec...]
    pallas_call x0 -> x2, Pallas kernels: none -> 19.1 us  [the longest x1 15.6 us: gather(): pl.pallas_call(functools.partial(gather_kernel, n_pair, n_virt, parts), o...]
    unnamed x0 -> x16, local copies, waits for them, and re-layouts: none -> 7.88 us
  transfers between devices with their start and end apart: 2 -> 0, of which waited for: 2 -> 0; matrix products, arithmetic and copies ran while one was open for 0% -> 0% of each run, Pallas kernels for 0% -> 0%
where the time goes in v1:
time: 27.4 us; the launch traced here: 27 us
  Pallas kernels  19.1 us (70%)
  local copies, waits for them, and re-layouts  7.88 us (29%)
    pallas_call x1, Pallas kernels, gather(): pl.pallas_call(functools.partial(gather_kernel, n_pair, n_virt, parts), o...  15.6 us
    unnamed x16, local copies, waits for them, and re-layouts  7.88 us
    pallas_call x1, Pallas kernels, ladder(): pl.pallas_call(ladder_kernel, out_shape=jax.ShapeDtypeStruct((rows, ab),...  3.5 us

profile of v1, /device:TPU:0, one launch (start us, length us, event | category | flops | bytes accessed | tf_op | source)
XLA Modules:
  0.0 27.0 jit_solution(4858466409194272611)
XLA Ops:
  0.0 0.0 copy-start.1
  0.0 1.2 %copy-done.1 = f32[1024,256]{1,0:T(8,128)S(1)} copy-done((f32[1024,256]{1,0:T(8,128)S(1)}, f32[1024,256]{1,0:T(8,128)}, u32[]{:S(2)}) %copy-start.1) | copy-done | bytes 1048600
  1.2 0.0 copy-start.2
  1.2 1.0 %copy-done.2 = f32[1024,128]{1,0:T(8,128)S(1)} copy-done((f32[1024,128]{1,0:T(8,128)S(1)}, f32[1024,128]{1,0:T(8,128)}, u32[]{:S(2)}) %copy-start.2) | copy-done | bytes 524312
  2.3 0.0 copy-start.3
  2.3 0.7 %copy-done.3 = s32[1024]{0:T(1024)S(1)} copy-done((s32[1024]{0:T(1024)S(1)}, s32[1024]{0:T(1024)}, u32[]{:S(2)}) %copy-start.3) | copy-done | bytes 4120
  3.0 0.0 copy-start.4
  3.0 0.7 %copy-done.4 = s32[1024]{0:T(1024)S(1)} copy-done((s32[1024]{0:T(1024)S(1)}, s32[1024]{0:T(1024)}, u32[]{:S(2)}) %copy-start.4) | copy-done | bytes 4120
  3.6 0.0 copy-start.6
  3.6 0.7 %copy-done.6 = s32[1024]{0:T(1024)S(1)} copy-done((s32[1024]{0:T(1024)S(1)}, s32[1024]{0:T(1024)}, u32[]{:S(2)}) %copy-start.6) | copy-done | bytes 4120
  4.3 15.6 %pick_and_gather.1 = (f32[128,1024]{1,0:T(8,128)S(1)}, bf16[256,1024]{1,0:T(8,128)(2,1)S(1)}) custom-call(f32[1024,128]{1,0:T(8,128)S(1)} %copy-done.2, f32[1024,256]{1,0:T(8,128)S(1)} %copy-done.1, s32[8,128]{1,0:T(8,128)S(1)} %bitcast.5, s32[8,128]{1,0:T(8,128)S(1)} %bitcast.7, s32[8,128]{1,0:T(8,128)S(1)} %bitcast.3, s32[8,128]{1,0:T(8,128)S(1)} %bitcast.4), custom_call_target="tpu_custom_call" | custom-call | tf_op jit(solution)/shard_map/pick_and_gather/pallas_call | solution.py:169
  19.9 0.0 copy-start
  20.0 2.2 %copy-done = f32[1024,1024]{1,0:T(8,128)S(1)} copy-done((f32[1024,1024]{1,0:T(8,128)S(1)}, f32[1024,1024]{1,0:T(8,128)}, u32[]{:S(2)}) %copy-start) | copy-done | bytes 4194328
  22.1 0.0 copy-start.5
  22.1 0.7 %copy-done.5 = s32[1024]{0:T(1024)S(1)} copy-done((s32[1024]{0:T(1024)S(1)}, s32[1024]{0:T(1024)}, u32[]{:S(2)}) %copy-start.5) | copy-done | bytes 4120
  22.8 0.0 copy-start.7
  22.8 0.7 %copy-done.7 = s32[1024]{0:T(1024)S(1)} copy-done((s32[1024]{0:T(1024)S(1)}, s32[1024]{0:T(1024)}, u32[]{:S(2)}) %copy-start.7) | copy-done | bytes 4120
  23.5 3.5 %ladder.1 = f32[1024,1024]{1,0:T(8,128)} custom-call(f32[128,1024]{1,0:T(8,128)S(1)} %get-tuple-element.7.t_ref, bf16[256,1024]{1,0:T(8,128)(2,1)S(1)} %get-tuple-element.8.v_ref, s32[8,128]{1,0:T(8,128)S(1)} %bitcast.6, s32[8,128]{1,0:T(8,128)S(1)} %bitcast.8, f32[1024,1024]{1,0:T(8,128)S(1)} %copy-done), custom_call_target="tpu_custom_call" | custom-call | tf_op jit(solution)/shard_map/ladder/pallas_call | solution.py:220
Async XLA Ops:
  0.0 1.2 %copy-start.1 = (f32[1024,256]{1,0:T(8,128)S(1)}, f32[1024,256]{1,0:T(8,128)}, u32[]{:S(2)}) copy-start(f32[1024,256]{1,0:T(8,128)} %v_hbm.1) | copy-start | bytes 3145732
  1.2 1.0 %copy-start.2 = (f32[1024,128]{1,0:T(8,128)S(1)}, f32[1024,128]{1,0:T(8,128)}, u32[]{:S(2)}) copy-start(f32[1024,128]{1,0:T(8,128)} %t_hbm.1) | copy-start | bytes 1572868
  2.3 0.7 %copy-start.3 = (s32[1024]{0:T(1024)S(1)}, s32[1024]{0:T(1024)}, u32[]{:S(2)}) copy-start(s32[1024]{0:T(1024)} %param.11) | copy-start | bytes 12292
  3.0 0.7 %copy-start.4 = (s32[1024]{0:T(1024)S(1)}, s32[1024]{0:T(1024)}, u32[]{:S(2)}) copy-start(s32[1024]{0:T(1024)} %param.9) | copy-start | bytes 12292
  3.6 0.7 %copy-start.6 = (s32[1024]{0:T(1024)S(1)}, s32[1024]{0:T(1024)}, u32[]{:S(2)}) copy-start(s32[1024]{0:T(1024)} %param.10) | copy-start | bytes 12292
  19.9 2.2 %copy-start = (f32[1024,1024]{1,0:T(8,128)S(1)}, f32[1024,1024]{1,0:T(8,128)}, u32[]{:S(2)}) copy-start(f32[1024,1024]{1,0:T(8,128)} %r_ref.1) | copy-start | bytes 12582916
  22.1 0.7 %copy-start.5 = (s32[1024]{0:T(1024)S(1)}, s32[1024]{0:T(1024)}, u32[]{:S(2)}) copy-start(s32[1024]{0:T(1024)} %param.9) | copy-start | bytes 12292
  22.8 0.7 %copy-start.7 = (s32[1024]{0:T(1024)S(1)}, s32[1024]{0:T(1024)}, u32[]{:S(2)}) copy-start(s32[1024]{0:T(1024)} %param.10) | copy-start | bytes 12292

commit v2 on v1

v2 whole, which is shorter than its diff:
```python
import functools

import jax
import jax.numpy as jnp
from jax import lax
from jax.experimental import pallas as pl
from jax.experimental.pallas import tpu as pltpu
from jax.sharding import PartitionSpec as P

IRREPS = 8
LANES = 128
MESH = pl.DeviceIdType.MESH


def pieces(x):
    high = x.astype(jnp.bfloat16)
    low = (x - high.astype(jnp.float32)).astype(jnp.bfloat16)
    return high, low


def nth_other(n, me, step):
    flip = me // (n // 2)
    mine = me + flip * (n - 1 - 2 * me)
    other = step + (step + n - mine) // n
    return other + flip * (n - 1 - 2 * other)


def irrep_row(rows_ref, first, count):
    n = count // LANES
    return jnp.concatenate([rows_ref[pl.ds(first + k, 1), :] for k in range(n)], axis=1)


def pick(cd_row, values, own_row):
    width = values.shape[1]
    blocks = width // IRREPS
    block = lax.broadcasted_iota(jnp.int32, (blocks, width), 0)
    lane_block = lax.shift_right_logical(lax.broadcasted_iota(jnp.int32, (blocks, width), 1), 3)
    slabs = [
        jnp.where((block == lane_block) & (cd_row == g), jnp.float32(1), jnp.float32(0))
        for g in range(IRREPS)
    ]
    sorter = jnp.concatenate(slabs, axis=0).astype(jnp.bfloat16)
    high, low = pieces(values)
    across = (((1,), (1,)), ((), ()))
    if width == LANES:
        both = jnp.concatenate([high, low], axis=1)
        twice = jnp.concatenate([sorter, sorter], axis=1)
        by_irrep = lax.dot_general(twice, both, across, preferred_element_type=jnp.float32)
    else:
        by_irrep = lax.dot_general(
            sorter, high, across, preferred_element_type=jnp.float32
        ) + lax.dot_general(sorter, low, across, preferred_element_type=jnp.float32)
    chosen = by_irrep[:blocks]
    for g in range(1, IRREPS):
        chosen = jnp.where(own_row == g, by_irrep[g * blocks : (g + 1) * blocks], chosen)
    return chosen


def ladder_kernel(
    n_pair, n_virt, parts,
    t_hbm, v_hbm, r_hbm, pi_hbm, ai_hbm, cdt_hbm, cdv_hbm,
    out_ref,
    t_own, v_own, pi_ref, ai_ref, cdt_ref, cdv_ref, t_all, v_all, right_ref, column_ref,
    load_sem, t_send, t_recv, tf_send, v_send, v_recv, vf_send,
):
    p, v = lax.axis_index("pair"), lax.axis_index("virt")
    a, b = v // 2, v % 2
    c, k = p // 2, p % 2
    n_a, n_c = n_virt // 2, n_pair // 2
    rows, t_width = t_own.shape
    ab, v_width = v_own.shape
    t_blocks, v_blocks = t_width // IRREPS, v_width // IRREPS
    blocks = t_all.shape[0]

    barrier = pltpu.get_barrier_semaphore()

    def greet(dev):
        pl.semaphore_signal(barrier, inc=1, device_id=dev, device_id_type=MESH)

    far_a = [nth_other(n_a, a, s) for s in range(n_a - 1)]
    far_c = [nth_other(n_c, c, s) for s in range(n_c - 1)]
    for o in far_a:
        greet((p, o * 2 + b))
    greet((p, a * 2 + 1 - b))
    for o in far_c:
        greet((o * 2 + k, v))
    greet((c * 2 + 1 - k, v))

    loads = [
        pltpu.make_async_copy(src, dst, load_sem.at[n])
        for n, (src, dst) in enumerate(
            [
                (t_hbm, t_own), (cdt_hbm, cdt_ref), (pi_hbm, pi_ref),
                (v_hbm, v_own), (cdv_hbm, cdv_ref), (ai_hbm, ai_ref), (r_hbm, out_ref),
            ]
        )
    ]
    for load in loads:
        load.start()

    def copy(ref, owner, count, part, span, send, recv, dev):
        at = ref.at[pl.ds(pl.multiple_of(owner * count, count), count), pl.ds(part * span, span)]
        return pltpu.make_async_remote_copy(
            src_ref=at, dst_ref=at, send_sem=send, recv_sem=recv, device_id=dev, device_id_type=MESH
        )

    t_span, v_span = rows // parts, ab // parts

    def t_copy(owner, part, send, dev):
        return copy(t_all, owner, t_blocks, part, t_span, send, t_recv.at[owner * parts + part], dev)

    def v_copy(owner, part, send, dev):
        return copy(v_all, owner, v_blocks, part, v_span, send, v_recv.at[owner * parts + part], dev)

    for load in loads[:3]:
        load.wait()
    cdt_row = irrep_row(cdt_ref, v * t_width // LANES, t_width) if t_width % LANES == 0 else cdt_ref[pl.ds(v, 1), :]
    sent = []
    for h in range(parts):
        own = irrep_row(pi_ref, h * t_span // LANES, t_span)
        t_all[pl.ds(pl.multiple_of(v * t_blocks, t_blocks), t_blocks), h * t_span : (h + 1) * t_span] = pick(
            cdt_row, t_own[h * t_span : (h + 1) * t_span, :], own
        )
        if h == 0:
            pl.semaphore_wait(barrier, n_a + n_c)
        for s in reversed(range(n_a - 1)):
            sent.append(t_copy(v, h, t_send.at[s, h], (p, far_a[s] * 2 + b)))
            sent[-1].start()
        sent.append(t_copy(v, h, t_send.at[n_a - 1, h], (p, a * 2 + 1 - b)))
        sent[-1].start()

    for load in loads[3:6]:
        load.wait()
    cdv_row = irrep_row(cdv_ref, p * v_width // LANES, v_width) if v_width % LANES == 0 else cdv_ref[pl.ds(p, 1), :]
    for h in range(parts):
        own = irrep_row(ai_ref, h * v_span // LANES, v_span)
        v_all[pl.ds(pl.multiple_of(p * v_blocks, v_blocks), v_blocks), h * v_span : (h + 1) * v_span] = pick(
            cdv_row, v_own[h * v_span : (h + 1) * v_span, :], own
        )
        for s in reversed(range(n_c - 1)):
            sent.append(v_copy(p, h, v_send.at[s, h], (far_c[s] * 2 + k, v)))
            sent[-1].start()
        sent.append(v_copy(p, h, v_send.at[n_c - 1, h], (c * 2 + 1 - k, v)))
        sent[-1].start()

    for m in range(rows // LANES):
        labels = jnp.broadcast_to(pi_ref[m : m + 1, :], (LANES, LANES))
        column_ref[m * LANES : (m + 1) * LANES, :] = labels.T

    for h in range(parts):
        for s in range(n_a - 1):
            onward = t_copy(far_a[s] * 2 + b, h, tf_send.at[s, h], (p, a * 2 + 1 - b))
            onward.wait_recv()
            onward.start()
            sent.append(onward)
        for s in range(n_c - 1):
            onward = v_copy(far_c[s] * 2 + k, h, vf_send.at[s, h], (c * 2 + 1 - k, v))
            onward.wait_recv()
            onward.start()
            sent.append(onward)

    for h in range(parts):
        span = slice(h * v_span, (h + 1) * v_span)
        for o in range(n_c):
            v_copy(o * 2 + 1 - k, h, v_send.at[0, h], (p, v)).wait_recv()
        high, low = pieces(v_all[:, span])
        right_ref[:blocks, span] = high
        right_ref[blocks : 2 * blocks, span] = high
        right_ref[2 * blocks : 3 * blocks, span] = low
        right_ref[3 * blocks :, span] = low

    ab_row = irrep_row(ai_ref, 0, ab)
    loads[6].wait()
    for h in range(parts):
        for o in range(n_a):
            t_copy(o * 2 + 1 - b, h, t_send.at[0, h], (p, v)).wait_recv()
        for m in range(h * t_span // LANES, (h + 1) * t_span // LANES):
            at = slice(m * LANES, (m + 1) * LANES)
            high, low = pieces(t_all[:, at].T)
            left = jnp.concatenate([high, low, high, low], axis=1)
            total = jnp.dot(left, right_ref[...], preferred_element_type=jnp.float32)
            same = jnp.concatenate([column_ref[at, :]] * (ab // LANES), axis=1) == ab_row
            out_ref[at, :] += jnp.where(same, total, jnp.float32(0))
    for s in sent:
        s.wait_send()


def ladder(n_pair, n_virt, t, v, residual, pi, ai, cd, cdt, cdv):
    parts = 2
    rows, t_width = t.shape
    ab, v_width = v.shape
    blocks = cd // IRREPS
    vmem, dma = pltpu.VMEM, pltpu.SemaphoreType.DMA
    n_a, n_c = n_virt // 2, n_pair // 2
    operands = (t, v, residual, pi, ai, cdt, cdv)
    return pl.pallas_call(
        functools.partial(ladder_kernel, n_pair, n_virt, parts),
        out_shape=pltpu.VMEM((rows, ab), jnp.float32),
        in_specs=[pl.BlockSpec(memory_space=pltpu.HBM)] * len(operands),
        out_specs=pl.BlockSpec(memory_space=vmem),
        scratch_shapes=[
            vmem((rows, t_width), jnp.float32),
            vmem((ab, v_width), jnp.float32),
            vmem(pi.shape, jnp.int32),
            vmem(ai.shape, jnp.int32),
            vmem(cdt.shape, jnp.int32),
            vmem(cdv.shape, jnp.int32),
            vmem((blocks, rows), jnp.float32),
            vmem((blocks, ab), jnp.float32),
            vmem((4 * blocks, ab), jnp.bfloat16),
            vmem((rows, LANES), jnp.int32),
            dma((7,)),
            dma((n_a, parts)),
            dma((n_virt * parts,)),
            dma((max(n_a - 1, 1), parts)),
            dma((n_c, parts)),
            dma((n_pair * parts,)),
            dma((max(n_c - 1, 1), parts)),
        ],
        compiler_params=pltpu.CompilerParams(
            collective_id=0, has_side_effects=True, vmem_limit_bytes=24 * 1024 * 1024
        ),
        name="pick_gather_ladder",
    )(*[pltpu.with_memory_space_constraint(x, pltpu.HBM) for x in operands])


def write_kernel(parts, src, dst, sem):
    span = src.shape[0] // parts
    copies = [
        pltpu.make_async_copy(src.at[pl.ds(n * span, span), :], dst.at[pl.ds(n * span, span), :], sem.at[n])
        for n in range(parts)
    ]
    for c in copies:
        c.start()
    for c in copies:
        c.wait()


def write(x):
    parts = 8
    return pl.pallas_call(
        functools.partial(write_kernel, parts),
        out_shape=jax.ShapeDtypeStruct(x.shape, x.dtype),
        in_specs=[pl.BlockSpec(memory_space=pl.ANY)],
        out_specs=pl.BlockSpec(memory_space=pl.ANY),
        scratch_shapes=[pltpu.SemaphoreType.DMA((parts,))],
        name="write",
    )(x)


def solution(mesh):
    n_pair, n_virt = mesh.shape["pair"], mesh.shape["virt"]

    def shards(amplitudes, integrals, residual_in, pair_irrep, ab_irrep, cd_irrep):
        cd = cd_irrep.shape[0]
        pi, ai = pair_irrep.reshape(-1, LANES), ab_irrep.reshape(-1, LANES)

        def cd_rows(width):
            return cd_irrep.reshape(-1, LANES if width % LANES == 0 else width)

        return write(
            ladder(
                n_pair, n_virt, amplitudes, integrals, residual_in, pi, ai, cd,
                cd_rows(amplitudes.shape[1]), cd_rows(integrals.shape[1]),
            )
        )

    placed = (P("pair", "virt"), P("virt", "pair"), P("pair", "virt"), P("pair"), P("virt"), P())
    return jax.shard_map(
        shards, mesh=mesh, in_specs=placed, out_specs=P("pair", "virt"), check_vma=False
    )
```

time: 27.4 us -> 147 us (5.36)
  Pallas kernels: 19.1 us -> 145 us
  local copies, waits for them, and re-layouts: 7.88 us -> 1.93 us
    pallas_call x2, Pallas kernels: 19.1 us -> 145 us  [the longest x1 128 us: write(): pl.pallas_call(functools.partial(write_kernel, parts), out_shape=jax.Shap...]
    unnamed x16 -> x2, local copies, waits for them, and re-layouts: 7.88 us -> 1.93 us
where the time goes in v2:
time: 147 us; the launch traced here: 146 us
  Pallas kernels  145 us (99%)
  local copies, waits for them, and re-layouts  1.93 us (1%)
    pallas_call x1, Pallas kernels, write(): pl.pallas_call(functools.partial(write_kernel, parts), out_shape=jax.Shap...  128 us
    pallas_call x1, Pallas kernels, ladder(): pl.pallas_call(functools.partial(ladder_kernel, n_pair, n_virt, parts), o...  16.3 us

profile of v2, /device:TPU:0, one launch (start us, length us, event | category | flops | bytes accessed | tf_op | source)
XLA Modules:
  0.0 146.5 jit_solution(5636085150463964190)
XLA Ops:
  0.0 16.3 %pick_gather_ladder.1.src = f32[1024,1024]{1,0:T(8,128)S(1)} custom-call(f32[1024,128]{1,0:T(8,128)} %t_hbm.1, f32[1024,256]{1,0:T(8,128)} %v_hbm.1, f32[1024,1024]{1,0:T(8,128)} %r_hbm.1, s32[8,128]{1,0:T(8,128)} %bitcast.5, s32[8,128]{1,0:T(8,128)} %bitcast.6, s32[8,128]{1,0:T(8,128)} %bitcast.3, s32[8,128]{1,0:T(8,128)} %bitcast.4), custom_call_target="tpu_custom_call" | custom-call | tf_op jit(solution)/shard_map/pick_gather_ladder/pallas_call | solution.py:196
  16.3 0.0 copy-start
  16.3 1.9 %copy-done = f32[1024,1024]{1,0:T(8,128)} copy-done((f32[1024,1024]{1,0:T(8,128)}, f32[1024,1024]{1,0:T(8,128)S(1)}, u32[]{:S(2)}) %copy-start) | copy-done | bytes 4194328
  18.2 128.2 %write.1 = f32[1024,1024]{1,0:T(8,128)} custom-call(f32[1024,1024]{1,0:T(8,128)} %copy-done), custom_call_target="tpu_custom_call" | custom-call | tf_op jit(solution)/shard_map/write/pallas_call | solution.py:241
Async XLA Ops:
  16.3 1.9 %copy-start = (f32[1024,1024]{1,0:T(8,128)}, f32[1024,1024]{1,0:T(8,128)S(1)}, u32[]{:S(2)}) copy-start(f32[1024,1024]{1,0:T(8,128)S(1)} %pick_gather_ladder.1.src) | copy-start | bytes 12582916

commit v3 on v2

--- a/solution.py
+++ b/solution.py
@@ -244,8 +244,9 @@
         in_specs=[pl.BlockSpec(memory_space=pl.ANY)],
         out_specs=pl.BlockSpec(memory_space=pl.ANY),
         scratch_shapes=[pltpu.SemaphoreType.DMA((parts,))],
+        compiler_params=pltpu.CompilerParams(vmem_limit_bytes=1024 * 1024),
         name="write",
-    )(x)
+    )(pltpu.with_memory_space_constraint(x, pltpu.VMEM))
 
 
 def solution(mesh):

time: 147 us -> 18.5 us (0.13)
  Pallas kernels: 145 us -> 18.4 us
  local copies, waits for them, and re-layouts: 1.93 us -> 0 us
    pallas_call x1, Pallas kernels: 128 us -> 2.07 us  [write(): pl.pallas_call(functools.partial(write_kernel, parts), out_shape=jax.Shap...]
    unnamed x2 -> x0, local copies, waits for them, and re-layouts: 1.93 us -> none
where the time goes in v3:
time: 18.5 us; the launch traced here: 18.4 us
  Pallas kernels  18.4 us (99%)
    pallas_call x1, Pallas kernels, ladder(): pl.pallas_call(functools.partial(ladder_kernel, n_pair, n_virt, parts), o...  16.3 us
    pallas_call x1, Pallas kernels, write(): pl.pallas_call(functools.partial(write_kernel, parts), out_shape=jax.Shap...  2.07 us

profile of v3, /device:TPU:0, one launch (start us, length us, event | category | flops | bytes accessed | tf_op | source)
XLA Modules:
  0.0 18.4 jit_solution(836971072227663112)
XLA Ops:
  0.0 16.3 %pick_gather_ladder.1.src = f32[1024,1024]{1,0:T(8,128)S(1)} custom-call(f32[1024,128]{1,0:T(8,128)} %t_hbm.1, f32[1024,256]{1,0:T(8,128)} %v_hbm.1, f32[1024,1024]{1,0:T(8,128)} %r_hbm.1, s32[8,128]{1,0:T(8,128)} %bitcast.5, s32[8,128]{1,0:T(8,128)} %bitcast.6, s32[8,128]{1,0:T(8,128)} %bitcast.3, s32[8,128]{1,0:T(8,128)} %bitcast.4), custom_call_target="tpu_custom_call" | custom-call | tf_op jit(solution)/shard_map/pick_gather_ladder/pallas_call | solution.py:196
  16.3 2.1 %write.1 = f32[1024,1024]{1,0:T(8,128)} custom-call(f32[1024,1024]{1,0:T(8,128)S(1)} %pick_gather_ladder.1.src), custom_call_target="tpu_custom_call" | custom-call | tf_op jit(solution)/shard_map/write/pallas_call | solution.py:241

commit v4 on v2

--- a/solution.py
+++ b/solution.py
@@ -56,11 +56,19 @@
     return chosen
 
 
+def tile(t_cols, right, column, ab_row, residual):
+    high, low = pieces(t_cols.T)
+    left = jnp.concatenate([high, low, high, low], axis=1)
+    total = jnp.dot(left, right, preferred_element_type=jnp.float32)
+    same = jnp.concatenate([column] * (ab_row.shape[1] // LANES), axis=1) == ab_row
+    return residual + jnp.where(same, total, jnp.float32(0))
+
+
 def ladder_kernel(
     n_pair, n_virt, parts,
     t_hbm, v_hbm, r_hbm, pi_hbm, ai_hbm, cdt_hbm, cdv_hbm,
-    out_ref,
-    t_own, v_own, pi_ref, ai_ref, cdt_ref, cdv_ref, t_all, v_all, right_ref, column_ref,
+    out_ref, t_last, right_ref, column_last, ai_ref,
+    t_own, v_own, pi_ref, cdt_ref, cdv_ref, t_all, v_all, column_ref,
     load_sem, t_send, t_recv, tf_send, v_send, v_recv, vf_send,
 ):
     p, v = lax.axis_index("pair"), lax.axis_index("virt")
@@ -143,10 +151,6 @@
         sent.append(v_copy(p, h, v_send.at[n_c - 1, h], (c * 2 + 1 - k, v)))
         sent[-1].start()
 
-    for m in range(rows // LANES):
-        labels = jnp.broadcast_to(pi_ref[m : m + 1, :], (LANES, LANES))
-        column_ref[m * LANES : (m + 1) * LANES, :] = labels.T
-
     for h in range(parts):
         for s in range(n_a - 1):
             onward = t_copy(far_a[s] * 2 + b, h, tf_send.at[s, h], (p, a * 2 + 1 - b))
@@ -159,6 +163,14 @@
             onward.start()
             sent.append(onward)
 
+    early = rows - t_span
+    for m in range(rows // LANES):
+        labels = jnp.broadcast_to(pi_ref[m : m + 1, :], (LANES, LANES)).T
+        if m * LANES < early:
+            column_ref[m * LANES : (m + 1) * LANES, :] = labels
+        else:
+            column_last[m * LANES - early : (m + 1) * LANES - early, :] = labels
+
     for h in range(parts):
         span = slice(h * v_span, (h + 1) * v_span)
         for o in range(n_c):
@@ -174,13 +186,12 @@
     for h in range(parts):
         for o in range(n_a):
             t_copy(o * 2 + 1 - b, h, t_send.at[0, h], (p, v)).wait_recv()
+        if h == parts - 1:
+            t_last[...] = t_all[:, early:]
+            break
         for m in range(h * t_span // LANES, (h + 1) * t_span // LANES):
             at = slice(m * LANES, (m + 1) * LANES)
-            high, low = pieces(t_all[:, at].T)
-            left = jnp.concatenate([high, low, high, low], axis=1)
-            total = jnp.dot(left, right_ref[...], preferred_element_type=jnp.float32)
-            same = jnp.concatenate([column_ref[at, :]] * (ab // LANES), axis=1) == ab_row
-            out_ref[at, :] += jnp.where(same, total, jnp.float32(0))
+            out_ref[at, :] = tile(t_all[:, at], right_ref[...], column_ref[at, :], ab_row, out_ref[at, :])
     for s in sent:
         s.wait_send()
 
@@ -195,19 +206,23 @@
     operands = (t, v, residual, pi, ai, cdt, cdv)
     return pl.pallas_call(
         functools.partial(ladder_kernel, n_pair, n_virt, parts),
-        out_shape=pltpu.VMEM((rows, ab), jnp.float32),
+        out_shape=(
+            vmem((rows, ab), jnp.float32),
+            vmem((blocks, rows // parts), jnp.float32),
+            vmem((4 * blocks, ab), jnp.bfloat16),
+            vmem((rows // parts, LANES), jnp.int32),
+            vmem(ai.shape, jnp.int32),
+        ),
         in_specs=[pl.BlockSpec(memory_space=pltpu.HBM)] * len(operands),
-        out_specs=pl.BlockSpec(memory_space=vmem),
+        out_specs=(pl.BlockSpec(memory_space=vmem),) * 5,
         scratch_shapes=[
             vmem((rows, t_width), jnp.float32),
             vmem((ab, v_width), jnp.float32),
             vmem(pi.shape, jnp.int32),
-            vmem(ai.shape, jnp.int32),
             vmem(cdt.shape, jnp.int32),
             vmem(cdv.shape, jnp.int32),
             vmem((blocks, rows), jnp.float32),
             vmem((blocks, ab), jnp.float32),
-            vmem((4 * blocks, ab), jnp.bfloat16),
             vmem((rows, LANES), jnp.int32),
             dma((7,)),
             dma((n_a, parts)),
@@ -224,28 +239,46 @@
     )(*[pltpu.with_memory_space_constraint(x, pltpu.HBM) for x in operands])
 
 
-def write_kernel(parts, src, dst, sem):
-    span = src.shape[0] // parts
+def finish_kernel(parts, done, t_last, right_ref, column_last, ai_ref, dst, late, sem):
+    rows, ab = done.shape
+    late_rows = late.shape[0]
+    early = rows - late_rows
+    span = early // parts
     copies = [
-        pltpu.make_async_copy(src.at[pl.ds(n * span, span), :], dst.at[pl.ds(n * span, span), :], sem.at[n])
+        pltpu.make_async_copy(done.at[pl.ds(n * span, span), :], dst.at[pl.ds(n * span, span), :], sem.at[n])
         for n in range(parts)
     ]
     for c in copies:
         c.start()
+    ab_row = irrep_row(ai_ref, 0, ab)
+    for m in range(late_rows // LANES):
+        at = slice(m * LANES, (m + 1) * LANES)
+        row = early + m * LANES
+        late[at, :] = tile(t_last[:, at], right_ref[...], column_last[at, :], ab_row, done[row : row + LANES, :])
+        copies.append(
+            pltpu.make_async_copy(late.at[pl.ds(m * LANES, LANES), :], dst.at[pl.ds(row, LANES), :], sem.at[parts + m])
+        )
+        copies[-1].start()
     for c in copies:
         c.wait()
 
 
-def write(x):
-    parts = 8
+def finish(done, t_last, *others):
+    parts = 4
+    late_rows = t_last.shape[1]
+    operands = (done, t_last, *others)
     return pl.pallas_call(
-        functools.partial(write_kernel, parts),
-        out_shape=jax.ShapeDtypeStruct(x.shape, x.dtype),
-        in_specs=[pl.BlockSpec(memory_space=pl.ANY)],
-        out_specs=pl.BlockSpec(memory_space=pl.ANY),
-        scratch_shapes=[pltpu.SemaphoreType.DMA((parts,))],
-        name="write",
-    )(x)
+        functools.partial(finish_kernel, parts),
+        out_shape=jax.ShapeDtypeStruct(done.shape, done.dtype),
+        in_specs=[pl.BlockSpec(memory_space=pltpu.VMEM)] * len(operands),
+        out_specs=pl.BlockSpec(memory_space=pltpu.HBM),
+        scratch_shapes=[
+            pltpu.VMEM((late_rows, done.shape[1]), done.dtype),
+            pltpu.SemaphoreType.DMA((parts + late_rows // LANES,)),
+        ],
+        compiler_params=pltpu.CompilerParams(vmem_limit_bytes=8 * 1024 * 1024),
+        name="finish",
+    )(*[pltpu.with_memory_space_constraint(x, pltpu.VMEM) for x in operands])
 
 
 def solution(mesh):
@@ -258,8 +291,8 @@
         def cd_rows(width):
             return cd_irrep.reshape(-1, LANES if width % LANES == 0 else width)
 
-        return write(
-            ladder(
+        return finish(
+            *ladder(
                 n_pair, n_virt, amplitudes, integrals, residual_in, pi, ai, cd,
                 cd_rows(amplitudes.shape[1]), cd_rows(integrals.shape[1]),
             )

time: 147 us -> 17.8 us (0.12)
  Pallas kernels: 145 us -> 17.6 us
  local copies, waits for them, and re-layouts: 1.93 us -> 0 us
    pallas_call x1, Pallas kernels: 128 us -> 2.07 us  [finish(): pl.pallas_call(functools.partial(finish_kernel, parts), out_shape=jax.Sha...]
    unnamed x2 -> x0, local copies, waits for them, and re-layouts: 1.93 us -> none
where the time goes in v4:
time: 17.8 us; the launch traced here: 17.6 us
  Pallas kernels  17.6 us (99%)
    pallas_call x1, Pallas kernels, ladder(): pl.pallas_call(functools.partial(ladder_kernel, n_pair, n_virt, parts), o...  15.5 us
    pallas_call x1, Pallas kernels, finish(): pl.pallas_call(functools.partial(finish_kernel, parts), out_shape=jax.Sha...  2.07 us

profile of v4, /device:TPU:0, one launch (start us, length us, event | category | flops | bytes accessed | tf_op | source)
XLA Modules:
  0.0 17.6 jit_solution(6388792296530688407)
XLA Ops:
  0.0 15.5 %pick_gather_ladder.1 = (f32[1024,1024]{1,0:T(8,128)S(1)}, f32[128,512]{1,0:T(8,128)S(1)}, bf16[512,1024]{1,0:T(8,128)(2,1)S(1)}, s32[512,128]{1,0:T(8,128)S(1)}, s32[8,128]{1,0:T(8,128)S(1)}) custom-call(f32[1024,128]{1,0:T(8,128)} %t_hbm.1, f32[1024,256]{1,0:T(8,128)} %v_hbm.1, f32[1024,1024]{1,0:T(8,128)} %r_hbm.1, s32[8,128]{1,0:T(8,128)} %bitcast.5, ...), custom_call_target="tpu_custom_call" | custom-call | tf_op jit(solution)/shard_map/pick_gather_ladder/pallas_call | solution.py:207
  15.6 2.1 %finish.1 = f32[1024,1024]{1,0:T(8,128)} custom-call(f32[1024,1024]{1,0:T(8,128)S(1)} %get-tuple-element.10.done, f32[128,512]{1,0:T(8,128)S(1)} %get-tuple-element.11.t_last, bf16[512,1024]{1,0:T(8,128)(2,1)S(1)} %get-tuple-element.12.right_ref, s32[512,128]{1,0:T(8,128)S(1)} %get-tuple-element.13.column_last, s32[8,128]{1,0:T(8,128)S(1)} %get-tuple-element.14.ai_ref), custom_call_target="tpu_custom_call" | custom-call | tf_op jit(solution)/shard_map/finish/pallas_call | solution.py:270

commit v5 on v4

--- a/solution.py
+++ b/solution.py
@@ -65,11 +65,11 @@
 
 
 def ladder_kernel(
-    n_pair, n_virt, parts,
+    n_pair, n_virt, parts, v_parts,
     t_hbm, v_hbm, r_hbm, pi_hbm, ai_hbm, cdt_hbm, cdv_hbm,
     out_ref, t_last, right_ref, column_last, ai_ref,
     t_own, v_own, pi_ref, cdt_ref, cdv_ref, t_all, v_all, column_ref,
-    load_sem, t_send, t_recv, tf_send, v_send, v_recv, vf_send,
+    load_sem, t_send, t_recv, tf_send, tr_send, v_send, v_recv, vf_send,
 ):
     p, v = lax.axis_index("pair"), lax.axis_index("virt")
     a, b = v // 2, v % 2
@@ -85,14 +85,21 @@
     def greet(dev):
         pl.semaphore_signal(barrier, inc=1, device_id=dev, device_id_type=MESH)
 
-    far_a = [nth_other(n_a, a, s) for s in range(n_a - 1)]
+    upper = a // (n_a // 2)
+    near, far = a + 1 - 2 * upper, a - 1 + 2 * upper
+    middle = jnp.logical_and(a > 0, a < n_a - 1)
+    others = [nth_other(n_a, a, s) for s in range(n_a - 1)]
     far_c = [nth_other(n_c, c, s) for s in range(n_c - 1)]
-    for o in far_a:
-        greet((p, o * 2 + b))
-    greet((p, a * 2 + 1 - b))
+    across = (p, a * 2 + 1 - b)
+    greet((p, near * 2 + b))
+    greet(across)
     for o in far_c:
         greet((o * 2 + k, v))
     greet((c * 2 + 1 - k, v))
+
+    @pl.when(middle)
+    def _():
+        greet((p, far * 2 + b))
 
     loads = [
         pltpu.make_async_copy(src, dst, load_sem.at[n])
@@ -112,35 +119,36 @@
             src_ref=at, dst_ref=at, send_sem=send, recv_sem=recv, device_id=dev, device_id_type=MESH
         )
 
-    t_span, v_span = rows // parts, ab // parts
+    t_span, v_span = rows // parts, ab // v_parts
 
     def t_copy(owner, part, send, dev):
         return copy(t_all, owner, t_blocks, part, t_span, send, t_recv.at[owner * parts + part], dev)
 
     def v_copy(owner, part, send, dev):
-        return copy(v_all, owner, v_blocks, part, v_span, send, v_recv.at[owner * parts + part], dev)
+        return copy(v_all, owner, v_blocks, part, v_span, send, v_recv.at[owner * v_parts + part], dev)
 
     for load in loads[:3]:
         load.wait()
     cdt_row = irrep_row(cdt_ref, v * t_width // LANES, t_width) if t_width % LANES == 0 else cdt_ref[pl.ds(v, 1), :]
-    sent = []
+    sent, relayed = [], []
     for h in range(parts):
         own = irrep_row(pi_ref, h * t_span // LANES, t_span)
         t_all[pl.ds(pl.multiple_of(v * t_blocks, t_blocks), t_blocks), h * t_span : (h + 1) * t_span] = pick(
             cdt_row, t_own[h * t_span : (h + 1) * t_span, :], own
         )
         if h == 0:
-            pl.semaphore_wait(barrier, n_a + n_c)
-        for s in reversed(range(n_a - 1)):
-            sent.append(t_copy(v, h, t_send.at[s, h], (p, far_a[s] * 2 + b)))
-            sent[-1].start()
-        sent.append(t_copy(v, h, t_send.at[n_a - 1, h], (p, a * 2 + 1 - b)))
+            pl.semaphore_wait(barrier, n_c + 2 + middle.astype(jnp.int32))
+        sent.append(t_copy(v, h, t_send.at[0, h], across))
         sent[-1].start()
+        sent.append(t_copy(v, h, t_send.at[1, h], (p, near * 2 + b)))
+        sent[-1].start()
+        relayed.append(t_copy(v, h, t_send.at[2, h], (p, far * 2 + b)))
+        pl.when(middle)(relayed[-1].start)
 
     for load in loads[3:6]:
         load.wait()
     cdv_row = irrep_row(cdv_ref, p * v_width // LANES, v_width) if v_width % LANES == 0 else cdv_ref[pl.ds(p, 1), :]
-    for h in range(parts):
+    for h in range(v_parts):
         own = irrep_row(ai_ref, h * v_span // LANES, v_span)
         v_all[pl.ds(pl.multiple_of(p * v_blocks, v_blocks), v_blocks), h * v_span : (h + 1) * v_span] = pick(
             cdv_row, v_own[h * v_span : (h + 1) * v_span, :], own
@@ -151,19 +159,29 @@
         sent.append(v_copy(p, h, v_send.at[n_c - 1, h], (c * 2 + 1 - k, v)))
         sent[-1].start()
 
-    for h in range(parts):
-        for s in range(n_a - 1):
-            onward = t_copy(far_a[s] * 2 + b, h, tf_send.at[s, h], (p, a * 2 + 1 - b))
-            onward.wait_recv()
-            onward.start()
-            sent.append(onward)
+    def pass_v(h):
         for s in range(n_c - 1):
             onward = v_copy(far_c[s] * 2 + k, h, vf_send.at[s, h], (c * 2 + 1 - k, v))
             onward.wait_recv()
             onward.start()
             sent.append(onward)
 
-    early = rows - t_span
+    order = sorted((h + s, s, h) for h in range(parts) for s in range(n_a - 1))
+    for n, (_, s, h) in enumerate(order):
+        source = others[s]
+        onward = t_copy(source * 2 + b, h, tf_send.at[s, h], across)
+        onward.wait_recv()
+        beyond = a - 1 + 2 * ((a - source + n_a) // n_a)
+        relayed.append(t_copy(source * 2 + b, h, tr_send.at[s, h], (p, beyond * 2 + b)))
+        pl.when(middle)(relayed[-1].start)
+        onward.start()
+        sent.append(onward)
+        if n == 2 * len(order) // 3:
+            pass_v(0)
+    for h in range(1, v_parts):
+        pass_v(h)
+
+    early = rows - t_last.shape[1]
     for m in range(rows // LANES):
         labels = jnp.broadcast_to(pi_ref[m : m + 1, :], (LANES, LANES)).T
         if m * LANES < early:
@@ -171,7 +189,7 @@
         else:
             column_last[m * LANES - early : (m + 1) * LANES - early, :] = labels
 
-    for h in range(parts):
+    for h in range(v_parts):
         span = slice(h * v_span, (h + 1) * v_span)
         for o in range(n_c):
             v_copy(o * 2 + 1 - k, h, v_send.at[0, h], (p, v)).wait_recv()
@@ -186,18 +204,23 @@
     for h in range(parts):
         for o in range(n_a):
             t_copy(o * 2 + 1 - b, h, t_send.at[0, h], (p, v)).wait_recv()
-        if h == parts - 1:
-            t_last[...] = t_all[:, early:]
-            break
+        if h * t_span >= early:
+            t_last[:, h * t_span - early : (h + 1) * t_span - early] = t_all[:, h * t_span : (h + 1) * t_span]
+            continue
         for m in range(h * t_span // LANES, (h + 1) * t_span // LANES):
             at = slice(m * LANES, (m + 1) * LANES)
             out_ref[at, :] = tile(t_all[:, at], right_ref[...], column_ref[at, :], ab_row, out_ref[at, :])
     for s in sent:
         s.wait_send()
 
+    @pl.when(middle)
+    def _():
+        for s in relayed:
+            s.wait_send()
+
 
 def ladder(n_pair, n_virt, t, v, residual, pi, ai, cd, cdt, cdv):
-    parts = 2
+    parts, v_parts = 4, 2
     rows, t_width = t.shape
     ab, v_width = v.shape
     blocks = cd // IRREPS
@@ -205,12 +228,12 @@
     n_a, n_c = n_virt // 2, n_pair // 2
     operands = (t, v, residual, pi, ai, cdt, cdv)
     return pl.pallas_call(
-        functools.partial(ladder_kernel, n_pair, n_virt, parts),
+        functools.partial(ladder_kernel, n_pair, n_virt, parts, v_parts),
         out_shape=(
             vmem((rows, ab), jnp.float32),
-            vmem((blocks, rows // parts), jnp.float32),
+            vmem((blocks, rows // 2), jnp.float32),
             vmem((4 * blocks, ab), jnp.bfloat16),
-            vmem((rows // parts, LANES), jnp.int32),
+            vmem((rows // 2, LANES), jnp.int32),
             vmem(ai.shape, jnp.int32),
         ),
         in_specs=[pl.BlockSpec(memory_space=pltpu.HBM)] * len(operands),
@@ -225,12 +248,13 @@
             vmem((blocks, ab), jnp.float32),
             vmem((rows, LANES), jnp.int32),
             dma((7,)),
-            dma((n_a, parts)),
+            dma((3, parts)),
             dma((n_virt * parts,)),
             dma((max(n_a - 1, 1), parts)),
-            dma((n_c, parts)),
-            dma((n_pair * parts,)),
-            dma((max(n_c - 1, 1), parts)),
+            dma((max(n_a - 1, 1), parts)),
+            dma((n_c, v_parts)),
+            dma((n_pair * v_parts,)),
+            dma((max(n_c - 1, 1), v_parts)),
         ],
         compiler_params=pltpu.CompilerParams(
             collective_id=0, has_side_effects=True, vmem_limit_bytes=24 * 1024 * 1024

time: 17.8 us -> 20.2 us (1.13)
  Pallas kernels: 17.6 us -> 20.1 us
    pallas_call x1, Pallas kernels: 15.5 us -> 18 us  [ladder(): pl.pallas_call(functools.partial(ladder_kernel, n_pair, n_virt, parts, v_...]
where the time goes in v5:
time: 20.2 us; the launch traced here: 20.1 us
  Pallas kernels  20.1 us (100%)
    pallas_call x1, Pallas kernels, ladder(): pl.pallas_call(functools.partial(ladder_kernel, n_pair, n_virt, parts, v_...  18 us
    pallas_call x1, Pallas kernels, finish(): pl.pallas_call(functools.partial(finish_kernel, parts), out_shape=jax.Sha...  2.07 us

profile of v5, /device:TPU:0, one launch (start us, length us, event | category | flops | bytes accessed | tf_op | source)
XLA Modules:
  0.0 20.1 jit_solution(8529966329279251386)
XLA Ops:
  0.0 18.0 %pick_gather_ladder.1 = (f32[1024,1024]{1,0:T(8,128)S(1)}, f32[128,512]{1,0:T(8,128)S(1)}, bf16[512,1024]{1,0:T(8,128)(2,1)S(1)}, s32[512,128]{1,0:T(8,128)S(1)}, s32[8,128]{1,0:T(8,128)S(1)}) custom-call(f32[1024,128]{1,0:T(8,128)} %t_hbm.1, f32[1024,256]{1,0:T(8,128)} %v_hbm.1, f32[1024,1024]{1,0:T(8,128)} %r_hbm.1, s32[8,128]{1,0:T(8,128)} %bitcast.5, ...), custom_call_target="tpu_custom_call" | custom-call | tf_op jit(solution)/shard_map/pick_gather_ladder/pallas_call | solution.py:230
  18.0 2.1 %finish.1 = f32[1024,1024]{1,0:T(8,128)} custom-call(f32[1024,1024]{1,0:T(8,128)S(1)} %get-tuple-element.10.done, f32[128,512]{1,0:T(8,128)S(1)} %get-tuple-element.11.t_last, bf16[512,1024]{1,0:T(8,128)(2,1)S(1)} %get-tuple-element.12.right_ref, s32[512,128]{1,0:T(8,128)S(1)} %get-tuple-element.13.column_last, s32[8,128]{1,0:T(8,128)S(1)} %get-tuple-element.14.ai_ref), custom_call_target="tpu_custom_call" | custom-call | tf_op jit(solution)/shard_map/finish/pallas_call | solution.py:294

commit v6 on v4

--- a/solution.py
+++ b/solution.py
@@ -16,13 +16,6 @@
     high = x.astype(jnp.bfloat16)
     low = (x - high.astype(jnp.float32)).astype(jnp.bfloat16)
     return high, low
-
-
-def nth_other(n, me, step):
-    flip = me // (n // 2)
-    mine = me + flip * (n - 1 - 2 * me)
-    other = step + (step + n - mine) // n
-    return other + flip * (n - 1 - 2 * other)
 
 
 def irrep_row(rows_ref, first, count):
@@ -69,12 +62,9 @@
     t_hbm, v_hbm, r_hbm, pi_hbm, ai_hbm, cdt_hbm, cdv_hbm,
     out_ref, t_last, right_ref, column_last, ai_ref,
     t_own, v_own, pi_ref, cdt_ref, cdv_ref, t_all, v_all, column_ref,
-    load_sem, t_send, t_recv, tf_send, v_send, v_recv, vf_send,
+    load_sem, t_send, t_recv, v_send, v_recv,
 ):
     p, v = lax.axis_index("pair"), lax.axis_index("virt")
-    a, b = v // 2, v % 2
-    c, k = p // 2, p % 2
-    n_a, n_c = n_virt // 2, n_pair // 2
     rows, t_width = t_own.shape
     ab, v_width = v_own.shape
     t_blocks, v_blocks = t_width // IRREPS, v_width // IRREPS
@@ -85,14 +75,10 @@
     def greet(dev):
         pl.semaphore_signal(barrier, inc=1, device_id=dev, device_id_type=MESH)
 
-    far_a = [nth_other(n_a, a, s) for s in range(n_a - 1)]
-    far_c = [nth_other(n_c, c, s) for s in range(n_c - 1)]
-    for o in far_a:
-        greet((p, o * 2 + b))
-    greet((p, a * 2 + 1 - b))
-    for o in far_c:
-        greet((o * 2 + k, v))
-    greet((c * 2 + 1 - k, v))
+    t_peers = [(p, lax.rem(v + s, n_virt)) for s in range(1, n_virt)]
+    v_peers = [(lax.rem(p + s, n_pair), v) for s in range(1, n_pair)]
+    for dev in t_peers + v_peers:
+        greet(dev)
 
     loads = [
         pltpu.make_async_copy(src, dst, load_sem.at[n])
@@ -130,12 +116,10 @@
             cdt_row, t_own[h * t_span : (h + 1) * t_span, :], own
         )
         if h == 0:
-            pl.semaphore_wait(barrier, n_a + n_c)
-        for s in reversed(range(n_a - 1)):
-            sent.append(t_copy(v, h, t_send.at[s, h], (p, far_a[s] * 2 + b)))
+            pl.semaphore_wait(barrier, n_virt + n_pair - 2)
+        for s, dev in enumerate(t_peers):
+            sent.append(t_copy(v, h, t_send.at[s, h], dev))
             sent[-1].start()
-        sent.append(t_copy(v, h, t_send.at[n_a - 1, h], (p, a * 2 + 1 - b)))
-        sent[-1].start()
 
     for load in loads[3:6]:
         load.wait()
@@ -145,23 +129,9 @@
         v_all[pl.ds(pl.multiple_of(p * v_blocks, v_blocks), v_blocks), h * v_span : (h + 1) * v_span] = pick(
             cdv_row, v_own[h * v_span : (h + 1) * v_span, :], own
         )
-        for s in reversed(range(n_c - 1)):
-            sent.append(v_copy(p, h, v_send.at[s, h], (far_c[s] * 2 + k, v)))
+        for s, dev in enumerate(v_peers):
+            sent.append(v_copy(p, h, v_send.at[s, h], dev))
             sent[-1].start()
-        sent.append(v_copy(p, h, v_send.at[n_c - 1, h], (c * 2 + 1 - k, v)))
-        sent[-1].start()
-
-    for h in range(parts):
-        for s in range(n_a - 1):
-            onward = t_copy(far_a[s] * 2 + b, h, tf_send.at[s, h], (p, a * 2 + 1 - b))
-            onward.wait_recv()
-            onward.start()
-            sent.append(onward)
-        for s in range(n_c - 1):
-            onward = v_copy(far_c[s] * 2 + k, h, vf_send.at[s, h], (c * 2 + 1 - k, v))
-            onward.wait_recv()
-            onward.start()
-            sent.append(onward)
 
     early = rows - t_span
     for m in range(rows // LANES):
@@ -173,8 +143,8 @@
 
     for h in range(parts):
         span = slice(h * v_span, (h + 1) * v_span)
-        for o in range(n_c):
-            v_copy(o * 2 + 1 - k, h, v_send.at[0, h], (p, v)).wait_recv()
+        for owner, _ in v_peers:
+            v_copy(owner, h, v_send.at[0, h], (p, v)).wait_recv()
         high, low = pieces(v_all[:, span])
         right_ref[:blocks, span] = high
         right_ref[blocks : 2 * blocks, span] = high
@@ -184,8 +154,8 @@
     ab_row = irrep_row(ai_ref, 0, ab)
     loads[6].wait()
     for h in range(parts):
-        for o in range(n_a):
-            t_copy(o * 2 + 1 - b, h, t_send.at[0, h], (p, v)).wait_recv()
+        for _, owner in t_peers:
+            t_copy(owner, h, t_send.at[0, h], (p, v)).wait_recv()
         if h == parts - 1:
             t_last[...] = t_all[:, early:]
             break
@@ -202,7 +172,6 @@
     ab, v_width = v.shape
     blocks = cd // IRREPS
     vmem, dma = pltpu.VMEM, pltpu.SemaphoreType.DMA
-    n_a, n_c = n_virt // 2, n_pair // 2
     operands = (t, v, residual, pi, ai, cdt, cdv)
     return pl.pallas_call(
         functools.partial(ladder_kernel, n_pair, n_virt, parts),
@@ -225,12 +194,10 @@
             vmem((blocks, ab), jnp.float32),
             vmem((rows, LANES), jnp.int32),
             dma((7,)),
-            dma((n_a, parts)),
+            dma((n_virt - 1, parts)),
             dma((n_virt * parts,)),
-            dma((max(n_a - 1, 1), parts)),
-            dma((n_c, parts)),
+            dma((n_pair - 1, parts)),
             dma((n_pair * parts,)),
-            dma((max(n_c - 1, 1), parts)),
         ],
         compiler_params=pltpu.CompilerParams(
             collective_id=0, has_side_effects=True, vmem_limit_bytes=24 * 1024 * 1024

time: 17.8 us -> 19.9 us (1.12)
  Pallas kernels: 17.6 us -> 19.7 us
    pallas_call x1, Pallas kernels: 15.5 us -> 17.7 us  [ladder(): pl.pallas_call(functools.partial(ladder_kernel, n_pair, n_virt, parts), o...]
where the time goes in v6:
time: 19.9 us; the launch traced here: 19.7 us
  Pallas kernels  19.7 us (99%)
    pallas_call x1, Pallas kernels, ladder(): pl.pallas_call(functools.partial(ladder_kernel, n_pair, n_virt, parts), o...  17.7 us
    pallas_call x1, Pallas kernels, finish(): pl.pallas_call(functools.partial(finish_kernel, parts), out_shape=jax.Sha...  2.07 us

profile of v6, /device:TPU:0, one launch (start us, length us, event | category | flops | bytes accessed | tf_op | source)
XLA Modules:
  0.0 19.7 jit_solution(2071967708307136047)
XLA Ops:
  0.0 17.7 %pick_gather_ladder.1 = (f32[1024,1024]{1,0:T(8,128)S(1)}, f32[128,512]{1,0:T(8,128)S(1)}, bf16[512,1024]{1,0:T(8,128)(2,1)S(1)}, s32[512,128]{1,0:T(8,128)S(1)}, s32[8,128]{1,0:T(8,128)S(1)}) custom-call(f32[1024,128]{1,0:T(8,128)} %t_hbm.1, f32[1024,256]{1,0:T(8,128)} %v_hbm.1, f32[1024,1024]{1,0:T(8,128)} %r_hbm.1, s32[8,128]{1,0:T(8,128)} %bitcast.5, ...), custom_call_target="tpu_custom_call" | custom-call | tf_op jit(solution)/shard_map/pick_gather_ladder/pallas_call | solution.py:176
  17.7 2.1 %finish.1 = f32[1024,1024]{1,0:T(8,128)} custom-call(f32[1024,1024]{1,0:T(8,128)S(1)} %get-tuple-element.10.done, f32[128,512]{1,0:T(8,128)S(1)} %get-tuple-element.11.t_last, bf16[512,1024]{1,0:T(8,128)(2,1)S(1)} %get-tuple-element.12.right_ref, s32[512,128]{1,0:T(8,128)S(1)} %get-tuple-element.13.column_last, s32[8,128]{1,0:T(8,128)S(1)} %get-tuple-element.14.ai_ref), custom_call_target="tpu_custom_call" | custom-call | tf_op jit(solution)/shard_map/finish/pallas_call | solution.py:237

commit v7 on v4

--- a/solution.py
+++ b/solution.py
@@ -65,7 +65,7 @@
 
 
 def ladder_kernel(
-    n_pair, n_virt, parts,
+    n_pair, n_virt, parts, v_parts,
     t_hbm, v_hbm, r_hbm, pi_hbm, ai_hbm, cdt_hbm, cdv_hbm,
     out_ref, t_last, right_ref, column_last, ai_ref,
     t_own, v_own, pi_ref, cdt_ref, cdv_ref, t_all, v_all, column_ref,
@@ -94,17 +94,19 @@
         greet((o * 2 + k, v))
     greet((c * 2 + 1 - k, v))
 
-    loads = [
-        pltpu.make_async_copy(src, dst, load_sem.at[n])
-        for n, (src, dst) in enumerate(
-            [
-                (t_hbm, t_own), (cdt_hbm, cdt_ref), (pi_hbm, pi_ref),
-                (v_hbm, v_own), (cdv_hbm, cdv_ref), (ai_hbm, ai_ref), (r_hbm, out_ref),
-            ]
-        )
+    t_span, v_span = rows // parts, ab // v_parts
+
+    def load(src, dst, n):
+        copy = pltpu.make_async_copy(src, dst, load_sem.at[n])
+        copy.start()
+        return copy
+
+    labels = [load(cdt_hbm, cdt_ref, 0), load(pi_hbm, pi_ref, 1)]
+    t_loads = [
+        load(t_hbm.at[pl.ds(h * t_span, t_span), :], t_own.at[pl.ds(h * t_span, t_span), :], 5 + h)
+        for h in range(parts)
     ]
-    for load in loads:
-        load.start()
+    v_loads = [load(cdv_hbm, cdv_ref, 2), load(ai_hbm, ai_ref, 3), load(v_hbm, v_own, 4)]
 
     def copy(ref, owner, count, part, span, send, recv, dev):
         at = ref.at[pl.ds(pl.multiple_of(owner * count, count), count), pl.ds(part * span, span)]
@@ -112,35 +114,54 @@
             src_ref=at, dst_ref=at, send_sem=send, recv_sem=recv, device_id=dev, device_id_type=MESH
         )
 
-    t_span, v_span = rows // parts, ab // parts
-
     def t_copy(owner, part, send, dev):
         return copy(t_all, owner, t_blocks, part, t_span, send, t_recv.at[owner * parts + part], dev)
 
     def v_copy(owner, part, send, dev):
-        return copy(v_all, owner, v_blocks, part, v_span, send, v_recv.at[owner * parts + part], dev)
-
-    for load in loads[:3]:
-        load.wait()
+        return copy(v_all, owner, v_blocks, part, v_span, send, v_recv.at[owner * v_parts + part], dev)
+
+    def send_t(h):
+        mine = [t_copy(v, h, t_send.at[s, h], (p, far_a[s] * 2 + b)) for s in reversed(range(n_a - 1))]
+        beside = t_copy(v, h, t_send.at[n_a - 1, h], (p, a * 2 + 1 - b))
+        for one in [*mine, beside]:
+            one.start()
+        sent.append(beside)
+        return mine
+
+    def pass_t(h, steps):
+        for s in steps:
+            onward = t_copy(far_a[s] * 2 + b, h, tf_send.at[s, h], (p, a * 2 + 1 - b))
+            onward.wait_recv()
+            onward.start()
+            sent.append(onward)
+
+    def pass_v(h):
+        for s in range(n_c - 1):
+            onward = v_copy(far_c[s] * 2 + k, h, vf_send.at[s, h], (c * 2 + 1 - k, v))
+            onward.wait_recv()
+            onward.start()
+            sent.append(onward)
+
+    for one in labels:
+        one.wait()
     cdt_row = irrep_row(cdt_ref, v * t_width // LANES, t_width) if t_width % LANES == 0 else cdt_ref[pl.ds(v, 1), :]
-    sent = []
+    sent, flying = [], []
     for h in range(parts):
+        t_loads[h].wait()
         own = irrep_row(pi_ref, h * t_span // LANES, t_span)
         t_all[pl.ds(pl.multiple_of(v * t_blocks, t_blocks), t_blocks), h * t_span : (h + 1) * t_span] = pick(
             cdt_row, t_own[h * t_span : (h + 1) * t_span, :], own
         )
         if h == 0:
             pl.semaphore_wait(barrier, n_a + n_c)
-        for s in reversed(range(n_a - 1)):
-            sent.append(t_copy(v, h, t_send.at[s, h], (p, far_a[s] * 2 + b)))
-            sent[-1].start()
-        sent.append(t_copy(v, h, t_send.at[n_a - 1, h], (p, a * 2 + 1 - b)))
-        sent[-1].start()
-
-    for load in loads[3:6]:
-        load.wait()
+        if h < 2:
+            flying.append(send_t(h))
+
+    for one in v_loads:
+        one.wait()
+    load_r = load(r_hbm, out_ref, 5 + parts)
     cdv_row = irrep_row(cdv_ref, p * v_width // LANES, v_width) if v_width % LANES == 0 else cdv_ref[pl.ds(p, 1), :]
-    for h in range(parts):
+    for h in range(v_parts):
         own = irrep_row(ai_ref, h * v_span // LANES, v_span)
         v_all[pl.ds(pl.multiple_of(p * v_blocks, v_blocks), v_blocks), h * v_span : (h + 1) * v_span] = pick(
             cdv_row, v_own[h * v_span : (h + 1) * v_span, :], own
@@ -152,18 +173,18 @@
         sent[-1].start()
 
     for h in range(parts):
-        for s in range(n_a - 1):
-            onward = t_copy(far_a[s] * 2 + b, h, tf_send.at[s, h], (p, a * 2 + 1 - b))
-            onward.wait_recv()
-            onward.start()
-            sent.append(onward)
-        for s in range(n_c - 1):
-            onward = v_copy(far_c[s] * 2 + k, h, vf_send.at[s, h], (c * 2 + 1 - k, v))
-            onward.wait_recv()
-            onward.start()
-            sent.append(onward)
-
-    early = rows - t_span
+        pass_t(h, range(1))
+        if h + 2 < parts:
+            for one in flying[h]:
+                one.wait_send()
+            flying.append(send_t(h + 2))
+        else:
+            sent.extend(flying[h])
+        pass_t(h, range(1, n_a - 1))
+        if h % 2 == 1:
+            pass_v(h // 2)
+
+    early = rows - t_last.shape[1]
     for m in range(rows // LANES):
         labels = jnp.broadcast_to(pi_ref[m : m + 1, :], (LANES, LANES)).T
         if m * LANES < early:
@@ -171,7 +192,7 @@
         else:
             column_last[m * LANES - early : (m + 1) * LANES - early, :] = labels
 
-    for h in range(parts):
+    for h in range(v_parts):
         span = slice(h * v_span, (h + 1) * v_span)
         for o in range(n_c):
             v_copy(o * 2 + 1 - k, h, v_send.at[0, h], (p, v)).wait_recv()
@@ -182,13 +203,13 @@
         right_ref[3 * blocks :, span] = low
 
     ab_row = irrep_row(ai_ref, 0, ab)
-    loads[6].wait()
+    load_r.wait()
     for h in range(parts):
         for o in range(n_a):
             t_copy(o * 2 + 1 - b, h, t_send.at[0, h], (p, v)).wait_recv()
-        if h == parts - 1:
-            t_last[...] = t_all[:, early:]
-            break
+        if h * t_span >= early:
+            t_last[:, h * t_span - early : (h + 1) * t_span - early] = t_all[:, h * t_span : (h + 1) * t_span]
+            continue
         for m in range(h * t_span // LANES, (h + 1) * t_span // LANES):
             at = slice(m * LANES, (m + 1) * LANES)
             out_ref[at, :] = tile(t_all[:, at], right_ref[...], column_ref[at, :], ab_row, out_ref[at, :])
@@ -197,7 +218,7 @@
 
 
 def ladder(n_pair, n_virt, t, v, residual, pi, ai, cd, cdt, cdv):
-    parts = 2
+    parts, v_parts = 4, 2
     rows, t_width = t.shape
     ab, v_width = v.shape
     blocks = cd // IRREPS
@@ -205,12 +226,12 @@
     n_a, n_c = n_virt // 2, n_pair // 2
     operands = (t, v, residual, pi, ai, cdt, cdv)
     return pl.pallas_call(
-        functools.partial(ladder_kernel, n_pair, n_virt, parts),
+        functools.partial(ladder_kernel, n_pair, n_virt, parts, v_parts),
         out_shape=(
             vmem((rows, ab), jnp.float32),
-            vmem((blocks, rows // parts), jnp.float32),
+            vmem((blocks, rows // 2), jnp.float32),
             vmem((4 * blocks, ab), jnp.bfloat16),
-            vmem((rows // parts, LANES), jnp.int32),
+            vmem((rows // 2, LANES), jnp.int32),
             vmem(ai.shape, jnp.int32),
         ),
         in_specs=[pl.BlockSpec(memory_space=pltpu.HBM)] * len(operands),
@@ -224,13 +245,13 @@
             vmem((blocks, rows), jnp.float32),
             vmem((blocks, ab), jnp.float32),
             vmem((rows, LANES), jnp.int32),
-            dma((7,)),
+            dma((6 + parts,)),
             dma((n_a, parts)),
             dma((n_virt * parts,)),
             dma((max(n_a - 1, 1), parts)),
-            dma((n_c, parts)),
-            dma((n_pair * parts,)),
-            dma((max(n_c - 1, 1), parts)),
+            dma((n_c, v_parts)),
+            dma((n_pair * v_parts,)),
+            dma((max(n_c - 1, 1), v_parts)),
         ],
         compiler_params=pltpu.CompilerParams(
             collective_id=0, has_side_effects=True, vmem_limit_bytes=24 * 1024 * 1024

time: 17.8 us -> 18.8 us (1.056)
  Pallas kernels: 17.6 us -> 18.6 us
    pallas_call x1, Pallas kernels: 15.5 us -> 16.5 us  [ladder(): pl.pallas_call(functools.partial(ladder_kernel, n_pair, n_virt, parts, v_...]
where the time goes in v7:
time: 18.8 us; the launch traced here: 18.6 us
  Pallas kernels  18.6 us (99%)
    pallas_call x1, Pallas kernels, ladder(): pl.pallas_call(functools.partial(ladder_kernel, n_pair, n_virt, parts, v_...  16.5 us
    pallas_call x1, Pallas kernels, finish(): pl.pallas_call(functools.partial(finish_kernel, parts), out_shape=jax.Sha...  2.07 us

profile of v7, /device:TPU:0, one launch (start us, length us, event | category | flops | bytes accessed | tf_op | source)
XLA Modules:
  0.0 18.6 jit_solution(6384994464724092600)
XLA Ops:
  0.0 16.5 %pick_gather_ladder.1 = (f32[1024,1024]{1,0:T(8,128)S(1)}, f32[128,512]{1,0:T(8,128)S(1)}, bf16[512,1024]{1,0:T(8,128)(2,1)S(1)}, s32[512,128]{1,0:T(8,128)S(1)}, s32[8,128]{1,0:T(8,128)S(1)}) custom-call(f32[1024,128]{1,0:T(8,128)} %t_hbm.1, f32[1024,256]{1,0:T(8,128)} %v_hbm.1, f32[1024,1024]{1,0:T(8,128)} %r_hbm.1, s32[8,128]{1,0:T(8,128)} %bitcast.5, ...), custom_call_target="tpu_custom_call" | custom-call | tf_op jit(solution)/shard_map/pick_gather_ladder/pallas_call | solution.py:228
  16.5 2.1 %finish.1 = f32[1024,1024]{1,0:T(8,128)} custom-call(f32[1024,1024]{1,0:T(8,128)S(1)} %get-tuple-element.10.done, f32[128,512]{1,0:T(8,128)S(1)} %get-tuple-element.11.t_last, bf16[512,1024]{1,0:T(8,128)(2,1)S(1)} %get-tuple-element.12.right_ref, s32[512,128]{1,0:T(8,128)S(1)} %get-tuple-element.13.column_last, s32[8,128]{1,0:T(8,128)S(1)} %get-tuple-element.14.ai_ref), custom_call_target="tpu_custom_call" | custom-call | tf_op jit(solution)/shard_map/finish/pallas_call | solution.py:291

commit v8 on v7

--- a/solution.py
+++ b/solution.py
@@ -145,7 +145,7 @@
     for one in labels:
         one.wait()
     cdt_row = irrep_row(cdt_ref, v * t_width // LANES, t_width) if t_width % LANES == 0 else cdt_ref[pl.ds(v, 1), :]
-    sent, flying = [], []
+    sent = []
     for h in range(parts):
         t_loads[h].wait()
         own = irrep_row(pi_ref, h * t_span // LANES, t_span)
@@ -154,8 +154,7 @@
         )
         if h == 0:
             pl.semaphore_wait(barrier, n_a + n_c)
-        if h < 2:
-            flying.append(send_t(h))
+        sent.extend(send_t(h))
 
     for one in v_loads:
         one.wait()
@@ -173,16 +172,8 @@
         sent[-1].start()
 
     for h in range(parts):
-        pass_t(h, range(1))
-        if h + 2 < parts:
-            for one in flying[h]:
-                one.wait_send()
-            flying.append(send_t(h + 2))
-        else:
-            sent.extend(flying[h])
-        pass_t(h, range(1, n_a - 1))
-        if h % 2 == 1:
-            pass_v(h // 2)
+        pass_t(h, range(n_a - 1))
+        pass_v(h)
 
     early = rows - t_last.shape[1]
     for m in range(rows // LANES):
@@ -218,7 +209,7 @@
 
 
 def ladder(n_pair, n_virt, t, v, residual, pi, ai, cd, cdt, cdv):
-    parts, v_parts = 4, 2
+    parts, v_parts = 2, 2
     rows, t_width = t.shape
     ab, v_width = v.shape
     blocks = cd // IRREPS

time: 18.8 us -> 17.8 us (0.947)
  Pallas kernels: 18.6 us -> 17.6 us
    pallas_call x1, Pallas kernels: 16.5 us -> 15.5 us  [ladder(): pl.pallas_call(functools.partial(ladder_kernel, n_pair, n_virt, parts, v_...]
where the time goes in v8:
time: 17.8 us; the launch traced here: 17.6 us
  Pallas kernels  17.6 us (99%)
    pallas_call x1, Pallas kernels, ladder(): pl.pallas_call(functools.partial(ladder_kernel, n_pair, n_virt, parts, v_...  15.5 us
    pallas_call x1, Pallas kernels, finish(): pl.pallas_call(functools.partial(finish_kernel, parts), out_shape=jax.Sha...  2.07 us

profile of v8, /device:TPU:0, one launch (start us, length us, event | category | flops | bytes accessed | tf_op | source)
XLA Modules:
  0.0 17.6 jit_solution(7715771769954919812)
XLA Ops:
  0.0 15.5 %pick_gather_ladder.1 = (f32[1024,1024]{1,0:T(8,128)S(1)}, f32[128,512]{1,0:T(8,128)S(1)}, bf16[512,1024]{1,0:T(8,128)(2,1)S(1)}, s32[512,128]{1,0:T(8,128)S(1)}, s32[8,128]{1,0:T(8,128)S(1)}) custom-call(f32[1024,128]{1,0:T(8,128)} %t_hbm.1, f32[1024,256]{1,0:T(8,128)} %v_hbm.1, f32[1024,1024]{1,0:T(8,128)} %r_hbm.1, s32[8,128]{1,0:T(8,128)} %bitcast.5, ...), custom_call_target="tpu_custom_call" | custom-call | tf_op jit(solution)/shard_map/pick_gather_ladder/pallas_call | solution.py:219
  15.5 2.1 %finish.1 = f32[1024,1024]{1,0:T(8,128)} custom-call(f32[1024,1024]{1,0:T(8,128)S(1)} %get-tuple-element.10.done, f32[128,512]{1,0:T(8,128)S(1)} %get-tuple-element.11.t_last, bf16[512,1024]{1,0:T(8,128)(2,1)S(1)} %get-tuple-element.12.right_ref, s32[512,128]{1,0:T(8,128)S(1)} %get-tuple-element.13.column_last, s32[8,128]{1,0:T(8,128)S(1)} %get-tuple-element.14.ai_ref), custom_call_target="tpu_custom_call" | custom-call | tf_op jit(solution)/shard_map/finish/pallas_call | solution.py:282

commit v9 on v8

--- a/solution.py
+++ b/solution.py
@@ -146,7 +146,7 @@
         one.wait()
     cdt_row = irrep_row(cdt_ref, v * t_width // LANES, t_width) if t_width % LANES == 0 else cdt_ref[pl.ds(v, 1), :]
     sent = []
-    for h in range(parts):
+    def start_t(h):
         t_loads[h].wait()
         own = irrep_row(pi_ref, h * t_span // LANES, t_span)
         t_all[pl.ds(pl.multiple_of(v * t_blocks, t_blocks), t_blocks), h * t_span : (h + 1) * t_span] = pick(
@@ -156,11 +156,7 @@
             pl.semaphore_wait(barrier, n_a + n_c)
         sent.extend(send_t(h))
 
-    for one in v_loads:
-        one.wait()
-    load_r = load(r_hbm, out_ref, 5 + parts)
-    cdv_row = irrep_row(cdv_ref, p * v_width // LANES, v_width) if v_width % LANES == 0 else cdv_ref[pl.ds(p, 1), :]
-    for h in range(v_parts):
+    def start_v(h):
         own = irrep_row(ai_ref, h * v_span // LANES, v_span)
         v_all[pl.ds(pl.multiple_of(p * v_blocks, v_blocks), v_blocks), h * v_span : (h + 1) * v_span] = pick(
             cdv_row, v_own[h * v_span : (h + 1) * v_span, :], own
@@ -170,6 +166,15 @@
             sent[-1].start()
         sent.append(v_copy(p, h, v_send.at[n_c - 1, h], (c * 2 + 1 - k, v)))
         sent[-1].start()
+
+    start_t(0)
+    for one in v_loads:
+        one.wait()
+    load_r = load(r_hbm, out_ref, 5 + parts)
+    cdv_row = irrep_row(cdv_ref, p * v_width // LANES, v_width) if v_width % LANES == 0 else cdv_ref[pl.ds(p, 1), :]
+    start_v(0)
+    start_t(1)
+    start_v(1)
 
     for h in range(parts):
         pass_t(h, range(n_a - 1))
@@ -198,12 +203,11 @@
     for h in range(parts):
         for o in range(n_a):
             t_copy(o * 2 + 1 - b, h, t_send.at[0, h], (p, v)).wait_recv()
-        if h * t_span >= early:
-            t_last[:, h * t_span - early : (h + 1) * t_span - early] = t_all[:, h * t_span : (h + 1) * t_span]
-            continue
-        for m in range(h * t_span // LANES, (h + 1) * t_span // LANES):
-            at = slice(m * LANES, (m + 1) * LANES)
-            out_ref[at, :] = tile(t_all[:, at], right_ref[...], column_ref[at, :], ab_row, out_ref[at, :])
+        if h == 0:
+            at = slice(0, early)
+            out_ref[at, :] = tile(t_all[:, at], right_ref[...], column_ref[...], ab_row, out_ref[at, :])
+        first = max(h * t_span, early)
+        t_last[:, first - early : (h + 1) * t_span - early] = t_all[:, first : (h + 1) * t_span]
     for s in sent:
         s.wait_send()
 
@@ -220,9 +224,9 @@
         functools.partial(ladder_kernel, n_pair, n_virt, parts, v_parts),
         out_shape=(
             vmem((rows, ab), jnp.float32),
-            vmem((blocks, rows // 2), jnp.float32),
+            vmem((blocks, rows - rows // 4), jnp.float32),
             vmem((4 * blocks, ab), jnp.bfloat16),
-            vmem((rows // 2, LANES), jnp.int32),
+            vmem((rows - rows // 4, LANES), jnp.int32),
             vmem(ai.shape, jnp.int32),
         ),
         in_specs=[pl.BlockSpec(memory_space=pltpu.HBM)] * len(operands),
@@ -235,7 +239,7 @@
             vmem(cdv.shape, jnp.int32),
             vmem((blocks, rows), jnp.float32),
             vmem((blocks, ab), jnp.float32),
-            vmem((rows, LANES), jnp.int32),
+            vmem((rows // 4, LANES), jnp.int32),
             dma((6 + parts,)),
             dma((n_a, parts)),
             dma((n_virt * parts,)),
@@ -251,7 +255,7 @@
     )(*[pltpu.with_memory_space_constraint(x, pltpu.HBM) for x in operands])
 
 
-def finish_kernel(parts, done, t_last, right_ref, column_last, ai_ref, dst, late, sem):
+def finish_kernel(parts, tiles, done, t_last, right_ref, column_last, ai_ref, dst, late, sem):
     rows, ab = done.shape
     late_rows = late.shape[0]
     early = rows - late_rows
@@ -263,12 +267,13 @@
     for c in copies:
         c.start()
     ab_row = irrep_row(ai_ref, 0, ab)
-    for m in range(late_rows // LANES):
-        at = slice(m * LANES, (m + 1) * LANES)
-        row = early + m * LANES
-        late[at, :] = tile(t_last[:, at], right_ref[...], column_last[at, :], ab_row, done[row : row + LANES, :])
+    step = late.shape[0] // tiles
+    for m in range(tiles):
+        at = slice(m * step, (m + 1) * step)
+        row = early + m * step
+        late[at, :] = tile(t_last[:, at], right_ref[...], column_last[at, :], ab_row, done[row : row + step, :])
         copies.append(
-            pltpu.make_async_copy(late.at[pl.ds(m * LANES, LANES), :], dst.at[pl.ds(row, LANES), :], sem.at[parts + m])
+            pltpu.make_async_copy(late.at[pl.ds(m * step, step), :], dst.at[pl.ds(row, step), :], sem.at[parts + m])
         )
         copies[-1].start()
     for c in copies:
@@ -276,19 +281,19 @@
 
 
 def finish(done, t_last, *others):
-    parts = 4
+    parts, tiles = 2, 3
     late_rows = t_last.shape[1]
     operands = (done, t_last, *others)
     return pl.pallas_call(
-        functools.partial(finish_kernel, parts),
+        functools.partial(finish_kernel, parts, tiles),
         out_shape=jax.ShapeDtypeStruct(done.shape, done.dtype),
         in_specs=[pl.BlockSpec(memory_space=pltpu.VMEM)] * len(operands),
         out_specs=pl.BlockSpec(memory_space=pltpu.HBM),
         scratch_shapes=[
             pltpu.VMEM((late_rows, done.shape[1]), done.dtype),
-            pltpu.SemaphoreType.DMA((parts + late_rows // LANES,)),
+            pltpu.SemaphoreType.DMA((parts + tiles,)),
         ],
-        compiler_params=pltpu.CompilerParams(vmem_limit_bytes=8 * 1024 * 1024),
+        compiler_params=pltpu.CompilerParams(vmem_limit_bytes=12 * 1024 * 1024),
         name="finish",
     )(*[pltpu.with_memory_space_constraint(x, pltpu.VMEM) for x in operands])
 

time: 17.8 us -> 17.9 us (level)
  no operation moved by 1% of the time
where the time goes in v9:
time: 17.9 us; the launch traced here: 17.7 us
  Pallas kernels  17.7 us (99%)
    pallas_call x1, Pallas kernels, ladder(): pl.pallas_call(functools.partial(ladder_kernel, n_pair, n_virt, parts, v_...  15.5 us
    pallas_call x1, Pallas kernels, finish(): pl.pallas_call(functools.partial(finish_kernel, parts, tiles), out_shape=...  2.19 us

profile of v9, /device:TPU:0, one launch (start us, length us, event | category | flops | bytes accessed | tf_op | source)
XLA Modules:
  0.0 17.7 jit_solution(14674740141001766066)
XLA Ops:
  0.0 15.5 %pick_gather_ladder.1 = (f32[1024,1024]{1,0:T(8,128)S(1)}, f32[128,768]{1,0:T(8,128)S(1)}, bf16[512,1024]{1,0:T(8,128)(2,1)S(1)}, s32[768,128]{1,0:T(8,128)S(1)}, s32[8,128]{1,0:T(8,128)S(1)}) custom-call(f32[1024,128]{1,0:T(8,128)} %t_hbm.1, f32[1024,256]{1,0:T(8,128)} %v_hbm.1, f32[1024,1024]{1,0:T(8,128)} %r_hbm.1, s32[8,128]{1,0:T(8,128)} %bitcast.5, ...), custom_call_target="tpu_custom_call" | custom-call | tf_op jit(solution)/shard_map/pick_gather_ladder/pallas_call | solution.py:223
  15.6 2.2 %finish.1 = f32[1024,1024]{1,0:T(8,128)} custom-call(f32[1024,1024]{1,0:T(8,128)S(1)} %get-tuple-element.10.done, f32[128,768]{1,0:T(8,128)S(1)} %get-tuple-element.11.t_last, bf16[512,1024]{1,0:T(8,128)(2,1)S(1)} %get-tuple-element.12.right_ref, s32[768,128]{1,0:T(8,128)S(1)} %get-tuple-element.13.column_last, s32[8,128]{1,0:T(8,128)S(1)} %get-tuple-element.14.ai_ref), custom_call_target="tpu_custom_call" | custom-call | tf_op jit(solution)/shard_map/finish/pallas_call | solution.py:287
